TPU v7x, 32 devices: a whole 2x2x4 slice. The times are simulated.
32 devices in a mesh: groups: 2 (over x), inst: 2 (over core), tp: 8 (over z, y).
Axes of the slice: x: 2, y: 2, z: 4, core: 2. Of those that a mesh axis runs over, the one named last changes fastest.
Arguments:
- hidden_input: bfloat16 [4, 16, 8192], P(None, ('groups', 'inst')), parts along dimension 1, may hold values from -6 to 6
- input_norm_gain: bfloat16 [8192], replicated, may hold values from 0.25 to 1.75
- query_weight: bfloat16 [8192, 8192], P(None, 'tp'), may hold values from -0.0625 to 0.0625
- key_weight: bfloat16 [8192, 1024], P(None, 'tp'), may hold values from -0.0625 to 0.0625
- value_weight: bfloat16 [8192, 1024], P(None, 'tp'), may hold values from -0.0625 to 0.0625
- output_weight: bfloat16 [8192, 8192], P('tp'), may hold values from -0.09375 to 0.09375
- key_value_cache: bfloat16 [16, 512, 2048], P(('groups', 'inst'), 'tp'), parts along dimension 0, may hold values from -320 to 320
- lengths: int32 [16], P('groups'), parts along dimension 0, may hold values from 64 to 512, as said below
- leaving: int32 [4, 2], P('groups'), parts along dimension 0, may hold values from 0 to 3, as said below
- request_adapter_index: int32 [16], P('groups'), parts along dimension 0, may hold values from 0 to 31
- adapter_page_table: int32 [32], replicated, may hold values from 0 to 31, each once
- adapter_down_pages: bfloat16 [32, 8192, 64], P('inst', 'tp'), may hold values from -0.0625 to 0.0625
- adapter_up_pages: bfloat16 [32, 64, 8192], P('inst', None, 'tp'), may hold values from -0.75 to 0.75
Outputs:
- layer_out: bfloat16 [4, 16, 8192], P(None, ('groups', 'inst'), 'tp'), parts along dimension 1
There are 2 independent parts, one for each index of `groups`. A program takes and returns all parts, laid end to end along the dimension named above; an argument that names none is the same for every part. Nothing has to cross between parts.
Inputs may be any that keep to these rules, and one draw needn't show every extreme that they name: `lengths`: some request has exactly 512 cached positions. `leaving`: each row lists 2 different slots.
All inputs are finite; a program needn't handle non-finite values.
Results may differ from a plain program's by a relative error of at most 0.039.
Values may be sent and summed in bfloat16 or wider, within the bound.
A program may use at most 128 MiB of HBM per device.

v0:
```python
import math

import jax
import jax.numpy as jnp
from jax import lax
from jax.sharding import PartitionSpec as P

QUERY_HEADS = 64
KVH = 8
HEAD_SIZE = 128


THETA = 500000.0
ADAPTER_SCALE = 0.5
NEGATIVE = -1e30


def partner(block, axis, bit):
    count = lax.axis_size(axis)
    route = []
    for low in range(count):
        high = low | 1 << bit
        if high != low and high < count:
            route += [(low, high), (high, low)]
    return lax.ppermute(block, axis, route)


def combined_all(value, axis, combine):
    everything = jax.tree.map(
        lambda part, kind: lax.all_gather(part.astype(kind), axis),
        value,
        (jnp.bfloat16, jnp.bfloat16, jnp.bfloat16),
    )

    def take(k):
        return jax.tree.map(lambda part, own: part[k].astype(own.dtype), everything, value)

    return lax.fori_loop(
        1, lax.axis_size(axis), lambda k, so_far: combine(so_far, take(k)), take(0)
    )


def normalize(hidden, input_norm_gain):
    values = hidden.astype(jnp.float32)
    factor = lax.rsqrt(jnp.mean(values * values, axis=-1, keepdims=True) + 1e-05)
    return (values * factor * input_norm_gain.astype(jnp.float32)).astype(jnp.bfloat16)


def rotate(tensor, position):
    middle = tensor.shape[-1] // 2
    freqs = jnp.exp(
        jnp.arange(middle, dtype=jnp.float32) * (-2.0 * math.log(THETA) / tensor.shape[-1])
    )
    angles = position[..., None] * freqs
    cosine = jnp.cos(angles)
    sine_part = jnp.sin(angles)
    first = tensor[..., :middle]
    second = tensor[..., middle:]
    return jnp.concatenate(
        [first * cosine - second * sine_part, second * cosine + first * sine_part], axis=-1
    )


def combine(earlier, later):
    top_first, total_first, mixed_first = earlier
    top_second, total_second, mixed_second = later
    top = jnp.maximum(top_first, top_second)
    scale_first = jnp.exp(top_first - top)
    scale_second = jnp.exp(top_second - top)
    total = total_first * scale_first + total_second * scale_second
    mixed = mixed_first * scale_first[..., None] + mixed_second * scale_second[..., None]
    return (top, total, mixed)


def shards(
    hidden_input,
    input_norm_gain,
    query_weight,
    key_weight,
    value_weight,
    output_weight,
    key_value_cache,
    lengths,
    leaving,
    request_adapter_index,
    adapter_page_table,
    adapter_down_pages,
    adapter_up_pages,
):
    decode_steps, request_rows, width = hidden_input.shape
    device = lax.axis_index("tp")
    instance = lax.axis_index("inst")
    head_cols = query_weight.shape[1]
    local_heads = head_cols // HEAD_SIZE
    positions = key_value_cache.shape[1]
    kv_width = KVH * HEAD_SIZE
    group = QUERY_HEADS // KVH
    normed = normalize(hidden_input, input_norm_gain).reshape(decode_steps * request_rows, width)
    query_part = jnp.dot(normed, query_weight, preferred_element_type=jnp.float32).astype(
        jnp.bfloat16
    )
    key_part = jnp.dot(normed, key_weight, preferred_element_type=jnp.float32).astype(jnp.bfloat16)
    value_part = jnp.dot(normed, value_weight, preferred_element_type=jnp.float32).astype(
        jnp.bfloat16
    )
    query_all, key_all, value_all = (
        lax.all_gather(query_part, "tp", axis=1, tiled=True),
        lax.all_gather(key_part, "tp", axis=1, tiled=True),
        lax.all_gather(value_part, "tp", axis=1, tiled=True),
    )
    lengths_here = lax.dynamic_slice_in_dim(lengths, instance * request_rows, request_rows)
    new_pos = (lengths_here[None, :] + jnp.arange(decode_steps, dtype=jnp.int32)[:, None]).astype(
        jnp.float32
    )[:, :, None]
    query_rot = rotate(
        query_all.reshape(decode_steps, request_rows, QUERY_HEADS, HEAD_SIZE).astype(jnp.float32),
        new_pos,
    ).astype(jnp.bfloat16)
    query_rot = query_rot.reshape(decode_steps, request_rows, KVH, group, HEAD_SIZE)
    key_rot = rotate(
        key_all.reshape(decode_steps, request_rows, KVH, HEAD_SIZE).astype(jnp.float32), new_pos
    ).astype(jnp.bfloat16)
    value_new = value_all.reshape(decode_steps, request_rows, KVH, HEAD_SIZE)
    outgoing_slots = lax.dynamic_index_in_dim(leaving, instance, 0, keepdims=False)
    arriving = partner(key_value_cache[outgoing_slots], "inst", 0)
    cache_now = key_value_cache.at[outgoing_slots].set(arriving)
    pages = adapter_page_table[request_adapter_index]
    adapter_store_size = adapter_down_pages.shape[0]
    own_pages = lax.dynamic_slice_in_dim(pages, instance * request_rows, request_rows)
    partner_pages = lax.dynamic_slice_in_dim(pages, (1 - instance) * request_rows, request_rows)

    def select_pages(wanted):
        local_page_index = jnp.clip(
            wanted - instance * adapter_store_size, 0, adapter_store_size - 1
        )
        down_matrix_flat = adapter_down_pages[local_page_index].reshape(request_rows, -1)
        up_matrix_flat = adapter_up_pages[local_page_index].reshape(request_rows, -1)
        return (
            jnp.concatenate([down_matrix_flat, up_matrix_flat], axis=1),
            wanted // adapter_store_size == instance,
        )

    outgoing_pages, held_there = select_pages(partner_pages)
    outgoing_pages = jnp.where(held_there[:, None], outgoing_pages, jnp.zeros_like(outgoing_pages))
    arriving_pages = partner(outgoing_pages, "inst", 0)
    local_pages, held_here = select_pages(own_pages)
    fetched_pages = jnp.where(held_here[:, None], local_pages, arriving_pages)
    down_matrix_size = adapter_down_pages.shape[1] * adapter_down_pages.shape[2]
    down_matrix_rows = fetched_pages[:, :down_matrix_size].reshape(
        request_rows, adapter_down_pages.shape[1], adapter_down_pages.shape[2]
    )
    up_matrix_rows = fetched_pages[:, down_matrix_size:].reshape(
        request_rows, adapter_up_pages.shape[1], adapter_up_pages.shape[2]
    )
    keys = cache_now[:, :, :kv_width].reshape(request_rows, positions, KVH, HEAD_SIZE)
    values = cache_now[:, :, kv_width:].reshape(request_rows, positions, KVH, HEAD_SIZE)
    place = device * positions + jnp.arange(positions, dtype=jnp.int32)
    valid = place[None, :] < lengths_here[:, None]
    valid_b = valid[None, :, None, None, :]
    inverse = 1.0 / math.sqrt(HEAD_SIZE)
    cache_scores = (
        jnp.einsum("srkgd,rpkd->srkgp", query_rot, keys, preferred_element_type=jnp.float32)
        * inverse
    )
    cache_scores = jnp.where(valid_b, cache_scores, NEGATIVE)
    new_scores = (
        jnp.einsum("srkgd,trkd->srkgt", query_rot, key_rot, preferred_element_type=jnp.float32)
        * inverse
    )
    causal = (jnp.arange(decode_steps)[None, :] <= jnp.arange(decode_steps)[:, None]) & (
        device == 0
    )
    causal_b = causal[:, None, None, None, :]
    new_scores = jnp.where(causal_b, new_scores, NEGATIVE)
    top = jnp.maximum(cache_scores.max(-1), new_scores.max(-1))
    cache_weights = jnp.exp(cache_scores - top[..., None]) * valid_b.astype(jnp.float32)
    new_weights = jnp.exp(new_scores - top[..., None]) * causal_b.astype(jnp.float32)
    total = cache_weights.sum(-1) + new_weights.sum(-1)
    mixed = jnp.einsum(
        "srkgp,rpkd->srkgd",
        cache_weights.astype(jnp.bfloat16),
        values,
        preferred_element_type=jnp.float32,
    )
    mixed = mixed + jnp.einsum(
        "srkgt,trkd->srkgd",
        new_weights.astype(jnp.bfloat16),
        value_new,
        preferred_element_type=jnp.float32,
    )
    top = top.reshape(decode_steps, request_rows, QUERY_HEADS)
    total = total.reshape(decode_steps, request_rows, QUERY_HEADS)
    mixed = mixed.reshape(decode_steps, request_rows, QUERY_HEADS, HEAD_SIZE)
    top_all, total_all, mixed_all = combined_all((top, total, mixed), "tp", combine)
    first_head = device * local_heads
    total_own = lax.dynamic_slice_in_dim(total_all, first_head, local_heads, 2)
    mixed_own = lax.dynamic_slice_in_dim(mixed_all, first_head, local_heads, 2)
    attention_output = mixed_own / total_own[..., None]
    attention_output = attention_output.astype(jnp.bfloat16).reshape(
        decode_steps * request_rows, head_cols
    )
    base_part = jnp.dot(attention_output, output_weight, preferred_element_type=jnp.float32)
    shrink_part = jnp.einsum(
        "src,rck->srk",
        attention_output.reshape(decode_steps, request_rows, head_cols),
        down_matrix_rows,
        preferred_element_type=jnp.float32,
    )
    shrunk_output = lax.psum(shrink_part, "tp")
    base_output = lax.psum_scatter(
        base_part.astype(jnp.bfloat16), "tp", scatter_dimension=1, tiled=True
    ).astype(jnp.float32)
    shrunk_output = shrunk_output.astype(jnp.bfloat16)
    adapter_delta = jnp.einsum(
        "srk,rkd->srd", shrunk_output, up_matrix_rows, preferred_element_type=jnp.float32
    )
    return (
        base_output.reshape(decode_steps, request_rows, -1) + ADAPTER_SCALE * adapter_delta
    ).astype(jnp.bfloat16)


def solution(mesh):
    return jax.shard_map(
        shards,
        mesh=mesh,
        in_specs=(
            P(None, ("groups", "inst"), None),
            P(),
            P(None, "tp"),
            P(None, "tp"),
            P(None, "tp"),
            P("tp", None),
            P(("groups", "inst"), "tp", None),
            P("groups"),
            P("groups", None),
            P("groups"),
            P(),
            P("inst", "tp", None),
            P("inst", None, "tp"),
        ),
        out_specs=P(None, ("groups", "inst"), "tp"),
        check_vma=False,
    )
```

profile of v0, /device:TPU:0, one launch (start us, length us, event | category | flops | bytes accessed | tf_op | source)
XLA Modules:
  0.0 294.1 jit_solution(7932003923521305788)
XLA Ops:
  8.0 1.4 gather_fusion
  10.7 1.4 gather_fusion.4
  12.1 2.4 copy.67
  14.5 2.7 reshape.291
  17.2 3.0 %gather_fusion.5 = bf16[4,64,1024]{2,1,0:T(8,128)(2,1)} fusion(bf16[16,64,1024]{2,1,0:T(8,128)(2,1)} %param.27, s32[1024]{0:T(1024)S(1)} %get-tuple-element.226), kind=kCustom, calls=%fused_computation.5 | custom fusion | bytes 1048592 | tf_op jit(solution)/shard_map/gather | solution.py:137
  20.2 1.4 copy.93
  21.6 2.6 maximum_select_fusion.1
  26.7 8.0 %convolution_convert_fusion.1 = bf16[16,1024]{1,0:T(8,128)(2,1)S(1)} fusion(bf16[16,8192]{1,0:T(8,128)(2,1)S(1)} %reshape.283, bf16[8192,1024]{1,0:T(8,128)(2,1)} %param.17), kind=kOutput, calls=%fused_computation.29 | convolution fusion | flops 268451840 | bytes 17072128 | tf_op jit(solution)/shard_map/dot_general | solution.py:99
  34.7 32.5 %all_gather.21 = bf16[16,8192]{1,0:T(8,128)(2,1)S(1)} all-gather(bf16[16,1024]{1,0:T(8,128)(2,1)S(1)} %convolution_convert_fusion.1), channel_id=1, replica_groups=mesh['groups'=2,'inst'=2,'tp'=8] {'tp'}, dimensions={1}, use_global_device_ids=true | all-gather | bytes 294912 | tf_op jit(solution)/shard_map/all_gather | solution.py:107
  68.6 2.0 convolution_convert_fusion.3
  70.7 26.0 %all_gather.22 = bf16[16,1024]{1,0:T(8,128)(2,1)S(1)} all-gather(bf16[16,128]{1,0:T(8,128)(2,1)S(1)} %convolution_convert_fusion.3), channel_id=1, replica_groups=mesh['groups'=2,'inst'=2,'tp'=8] {'tp'}, dimensions={1}, use_global_device_ids=true | all-gather | bytes 36864 | tf_op jit(solution)/shard_map/all_gather | solution.py:108
  100.0 3.0 %gather_fusion.3 = bf16[4,64,1024]{2,1,0:T(8,128)(2,1)} fusion(bf16[16,64,1024]{2,1,0:T(8,128)(2,1)} %param.27, s32[1024]{0:T(1024)S(1)} %get-tuple-element.227), kind=kCustom, calls=%fused_computation.3 | custom fusion | bytes 1048592 | tf_op jit(solution)/shard_map/gather | solution.py:137
  104.1 26.0 %all_gather.25 = bf16[16,1024]{1,0:T(8,128)(2,1)S(1)} all-gather(bf16[16,128]{1,0:T(8,128)(2,1)S(1)} %convolution_convert_fusion.2), channel_id=1, replica_groups=mesh['groups'=2,'inst'=2,'tp'=8] {'tp'}, dimensions={1}, use_global_device_ids=true | all-gather | bytes 36864 | tf_op jit(solution)/shard_map/all_gather | solution.py:109
  131.3 1.5 copy.92
  133.0 2.2 fusion.58
  135.2 1.7 scatter_fusion
  141.3 30.5 %all_gather.24 = bf16[8,4,4,64]{3,2,1,0:T(4,128)(2,1)S(1)} all-gather(bf16[1,4,4,64]{3,2,1,0:T(4,128)(2,1)S(1)} %convert_element_type.191), channel_id=1, replica_groups=mesh['groups'=2,'inst'=2,'tp'=8] {'tp'}, dimensions={0}, use_global_device_ids=true | all-gather | bytes 18432 | tf_op jit(solution)/shard_map/all_gather | solution.py:30
  171.8 30.6 %all_gather.23 = bf16[8,4,4,64]{3,2,1,0:T(4,128)(2,1)S(1)} all-gather(bf16[1,4,4,64]{3,2,1,0:T(4,128)(2,1)S(1)} %convert_element_type.185), channel_id=1, replica_groups=mesh['groups'=2,'inst'=2,'tp'=8] {'tp'}, dimensions={0}, use_global_device_ids=true | all-gather | bytes 18432 | tf_op jit(solution)/shard_map/all_gather | solution.py:30
  202.4 1.9 maximum_select_fusion
  205.4 10.6 %while.19 = (s32[]{:T(128)}, f32[4,4,64]{2,1,0:T(4,128)S(1)}, f32[4,4,64]{2,1,0:T(4,128)S(1)}, f32[4,4,64,128]{3,2,1,0:T(8,128)S(1)}, bf16[8,4,4,64]{3,2,1,0:T(4...) while((s32[]{:T(128)}, f32[4,4,64]{2,1,0:T(4,128)S(1)}, ...), condition=%wide.region_7.8_spmd, body=%wide.region_6.7_spmd.sunk | while | flops 532485 | bytes 1347735 | solution.py:38
  205.5 1.5 fusion.71
  207.0 1.5 fusion.71
  208.5 1.5 fusion.71
  210.0 1.5 fusion.71
  211.5 1.5 fusion.71
  213.0 1.5 fusion.71
  214.5 1.5 fusion.71
  216.2 8.8 %convolution_convert_fusion = bf16[16,8192]{1,0:T(8,128)(2,1)} fusion(bf16[1024,8192]{1,0:T(8,128)(2,1)} %param.20, bf16[2,8,8,128]{3,2,1,0:T(8,128)(2,1)S(1)} %bitcast.138), kind=kOutput, calls=%fused_computation.15 | convolution fusion | flops 268566528 | bytes 17072128 | tf_op jit(solution)/shard_map/dot_general | solution.py:202
  226.4 1.9 reshape.294
  228.6 18.9 %psum.7 = bf16[4,4,64]{2,0,1:T(4,128)(2,1)S(1)} all-reduce(f32[4,4,64]{2,0,1:T(4,128)S(1)} %convolution_bitcast_fusion), channel_id=1, replica_groups=mesh['groups'=2,'inst'=2,'tp'=8] {'tp'}, use_global_device_ids=true, to_apply=%region_9.10 | all-reduce | flops 1024 | bytes 6144 | tf_op jit(solution)/shard_map/psum | solution.py:209
  247.5 36.9 %reduce-scatter.2.cloned.1.call-done = bf16[16,1024]{1,0:T(8,128)(2,1)} async-done(((bf16[16,8192]{1,0:T(8,128)(2,1)}), bf16[16,1024]{1,0:T(8,128)(2,1)}) %reduce-scatter.2.cloned.1.call-update) | async-done | bytes 32784 | tf_op jit(solution)/shard_map/reduce_scatter | solution.py:210
  285.2 1.4 fusion.11
  (108 shorter events, 21.1 us)
Async XLA Ops:
  6.5 4.2 %copy-start = (bf16[16,1024,64]{1,2,0:T(8,128)(2,1)S(1)}, bf16[16,1024,64]{1,2,0:T(8,128)(2,1)}, u32[]{:S(2)}) copy-start(bf16[16,1024,64]{1,2,0:T(8,128)(2,1)} %param.26) | copy-start | bytes 6291460
  6.5 1.4 copy-start.12
  6.5 3.3 %copy-start.13 = (s32[8]{0:T(128)S(1)}, s32[8]{0:T(128)}, u32[]{:S(2)}) copy-start(s32[8]{0:T(128)} %param.24) | copy-start | bytes 100
  6.5 3.3 %copy-start.2 = (s32[32]{0:T(128)S(1)}, s32[32]{0:T(128)}, u32[]{:S(2)}) copy-start(s32[32]{0:T(128)} %param.25) | copy-start | bytes 388
  6.5 197.9 %all-gather.2.cloned.1.call-start = ((), (), s32[]{:S(2)}) async-start(), calls=%async_computation.1 | async-start | bytes 2359296 | tf_op jit(solution)/shard_map/all_gather | solution.py:30
  9.4 125.8 %collective-permute-start = (bf16[2,64,2048]{2,1,0:T(8,128)(2,1)}, bf16[2,64,2048]{2,1,0:T(8,128)(2,1)}, u32[]{:S(2)}, u32[]{:S(2)}) collective-permute-start(bf16[2,64,2048]{2,1,0:T(8,128)(2,1)} %gather_fusion), channel_id=1, source_target_pairs={{0,8},{8,0},{1,9},{9,1},{2,10},{10,2},{3,11},{11,3},{4,12},{12,4},... | collective-permute-start | bytes 1572872 | tf_op jit(solution)/shard_map/ppermute | solution.py:25
  17.2 7.1 %copy-start.14 = (s32[8]{0:T(128)S(1)}, s32[8]{0:T(128)}, u32[]{:S(2)}) copy-start(s32[8]{0:T(128)} %param.22) | copy-start | bytes 100
  17.2 7.3 %copy-start.10 = (bf16[8192]{0:T(1024)(128)(2,1)S(1)}, bf16[8192]{0:T(1024)(128)(2,1)}, u32[]{:S(2)}) copy-start(bf16[8192]{0:T(1024)(128)(2,1)} %param.16) | copy-start | bytes 49156
  17.2 7.3 %copy-start.5 = (bf16[4,4,8192]{2,1,0:T(4,128)(2,1)S(1)}, bf16[4,4,8192]{2,1,0:T(4,128)(2,1)}, u32[]{:S(2)}) copy-start(bf16[4,4,8192]{2,1,0:T(4,128)(2,1)} %param.15) | copy-start | bytes 786436
  24.2 178.2 %collective-permute-start.1 = (bf16[4,131072]{1,0:T(4,128)(2,1)}, bf16[4,131072]{1,0:T(4,128)(2,1)}, u32[]{:S(2)}, u32[]{:S(2)}) collective-permute-start(bf16[4,131072]{1,0:T(4,128)(2,1)} %maximum_select_fusion.1), channel_id=1, source_target_pairs={{0,8},{8,0},{1,9},{9,1},{2,10},{10,2},{3,11},{11,3},{4,12},{12,4},... | collective-permute-start | bytes 3145736 | tf_op jit(solution)/shard_map/ppermute | solution.py:25
  68.1 28.7 %copy-start.4 = (bf16[8192,128]{1,0:T(8,128)(2,1)S(1)}, bf16[8192,128]{1,0:T(8,128)(2,1)}, u32[]{:S(2)}) copy-start(bf16[8192,128]{1,0:T(8,128)(2,1)} %param.19) | copy-start | bytes 6291460
  99.9 30.2 %copy-start.3 = (bf16[4,1024,64]{1,2,0:T(8,128)(2,1)S(1)}, bf16[4,1024,64]{1,2,0:T(8,128)(2,1)}, u32[]{:S(2)}) copy-start(bf16[4,1024,64]{1,2,0:T(8,128)(2,1)} %gather_fusion.2) | copy-start | bytes 1572868
  133.0 2.2 copy-start.6
  133.0 2.2 copy-start.8
  137.0 1.0 copy-start.7
  137.0 1.0 copy-start.9
  137.0 1.0 copy-start.11
  140.1 144.3 %reduce-scatter.2.cloned.1.call-start = ((), (), s32[]{:S(2)}) async-start(), calls=%async_computation.2 | async-start | bytes 294912 | tf_op jit(solution)/shard_map/reduce_scatter | solution.py:210
  225.0 62.3 %copy-start.1 = (bf16[16,1024,64]{1,2,0:T(8,128)(2,1)S(1)}, bf16[16,1024,64]{1,2,0:T(8,128)(2,1)}, u32[]{:S(2)}) copy-start(bf16[16,1024,64]{1,2,0:T(8,128)(2,1)} %param.26) | copy-start | bytes 6291460
Sparse Core Ops, SparseCore 0:
  140.2 47.4 all-gather.1
  225.1 59.2 reduce-scatter.1
where the time goes:
time: 295 us; the launch traced here: 294 us
  blocking collectives  165 us (56%)
  waiting for transfers between devices  37 us (13%)
  local copies, waits for them, and re-layouts  32.2 us (11%)
  matrix products  24.3 us (8%)
  other arithmetic  21.3 us (7%)
  between operations  13.8 us (5%)
    all_gather x2, blocking collectives, combined_all(): lax.all_gather(part.astype(kind), axis)  61.1 us
    reduce_scatter x1, waiting for transfers between devices, shards(): lax.psum_scatter(base_part.astype(jnp.bfloat16), 'tp', scatter_dimension=...  36.9 us
    all_gather x1, blocking collectives, shards(): lax.all_gather(query_part, 'tp', axis=1, tiled=True)  32.5 us
    all_gather x1, blocking collectives, shards(): lax.all_gather(key_part, 'tp', axis=1, tiled=True)  26 us
    all_gather x1, blocking collectives, shards(): lax.all_gather(value_part, 'tp', axis=1, tiled=True)  26 us
    psum x1, blocking collectives, shards(): shrunk_output = lax.psum(shrink_part, 'tp')  18.9 us
    add x7, other arithmetic, combine(): mixed_first * scale_first[..., None]  10.2 us
    dot_general x1, matrix products, shards(): jnp.dot(attention_output, output_weight, preferred_element_type=jnp.float32)  8.8 us
  transfers between devices with their start and end apart: 4, of which 1 were waited for; matrix products, arithmetic and copies ran while one was open for 17% of the time, Pallas kernels for 0%

commit v1 on v0

--- a/solution.py
+++ b/solution.py
@@ -1,13 +1,17 @@
+import functools
 import math
 
 import jax
 import jax.numpy as jnp
 from jax import lax
+from jax.experimental import pallas as pl
+from jax.experimental.pallas import tpu as pltpu
 from jax.sharding import PartitionSpec as P
 
 QUERY_HEADS = 64
 KVH = 8
 HEAD_SIZE = 128
+MESH = pl.DeviceIdType.MESH
 
 
 THETA = 500000.0
@@ -219,9 +223,507 @@
     ).astype(jnp.bfloat16)
 
 
+def fused_kernel(
+    dims,
+    hidden_ref,
+    gain_ref,
+    wq_hbm,
+    wk_hbm,
+    wv_hbm,
+    wo_hbm,
+    cache_hbm,
+    lengths_ref,
+    leaving_ref,
+    adapter_ref,
+    table_ref,
+    down_hbm,
+    up_hbm,
+    out_ref,
+    wq,
+    wk,
+    wv,
+    wo,
+    cache,
+    moved_out,
+    moved_in,
+    keys,
+    values,
+    down,
+    up,
+    down_out,
+    up_out,
+    down_in,
+    up_in,
+    hidden,
+    normed,
+    query_all,
+    part_out,
+    part_in,
+    stat,
+    stat_out,
+    stat_in,
+    shrink_part,
+    shrink_in,
+    base_out,
+    base_in,
+    wq_sem,
+    wkv_sem,
+    wo_sem,
+    store_sem,
+    pair_send,
+    pair_recv,
+    query_send,
+    query_recv,
+    part_send,
+    part_recv,
+    stat_send,
+    stat_recv,
+    shrink_send,
+    shrink_recv,
+    base_send,
+    base_recv,
+):
+    n, steps, reqs, width, head_cols, positions, store, rank, out_cols, chunks, pieces = dims
+    rows = steps * reqs
+    head_count = head_cols // HEAD_SIZE
+    chunk_heads = head_count // chunks
+    chunk_cols = chunk_heads * HEAD_SIZE
+    piece = width // pieces
+    kv_width = n * HEAD_SIZE
+    me = lax.axis_index("tp")
+    inst = lax.axis_index("inst")
+    other = 1 - inst
+    f32, bf16 = jnp.float32, jnp.bfloat16
+    inverse = 1.0 / math.sqrt(HEAD_SIZE)
+
+    def each_peer(body):
+        def step(o, carry):
+            body(lax.rem(me + 1 + o, n))
+            return carry
+
+        lax.fori_loop(0, n - 1, step, 0)
+
+    cache_copy = pltpu.make_async_copy(cache_hbm, cache, store_sem.at[0])
+    cache_copy.start()
+    wq_copies = {}
+    for c in range(chunks):
+        for k in range(pieces):
+            at = (pl.ds(k * piece, piece), pl.ds(c * chunk_cols, chunk_cols))
+            wq_copies[c, k] = pltpu.make_async_copy(
+                wq_hbm.at[at], wq.at[at], wq_sem.at[c, k]
+            )
+            wq_copies[c, k].start()
+    wk_copy = pltpu.make_async_copy(wk_hbm, wk, wkv_sem.at[0])
+    wv_copy = pltpu.make_async_copy(wv_hbm, wv, wkv_sem.at[1])
+    down_copy = pltpu.make_async_copy(down_hbm, down, store_sem.at[1])
+    up_copy = pltpu.make_async_copy(up_hbm, up, store_sem.at[2])
+    wk_copy.start()
+    wv_copy.start()
+    down_copy.start()
+    up_copy.start()
+
+    def wo_copy(p):
+        cols = pl.ds(pl.multiple_of(p * out_cols, out_cols), out_cols)
+        return pltpu.make_async_copy(wo_hbm.at[:, cols], wo.at[p], wo_sem.at[p])
+
+    def start_wo(o, carry):
+        wo_copy(lax.rem(me + 1 + o, n)).start()
+        return carry
+
+    lax.fori_loop(0, n, start_wo, 0)
+
+    barrier = pltpu.get_barrier_semaphore()
+    each_peer(lambda p: pl.semaphore_signal(barrier, inc=1, device_id={"tp": p}, device_id_type=MESH))
+    pl.semaphore_signal(barrier, inc=1, device_id={"inst": other}, device_id_type=MESH)
+
+    for s in range(steps):
+        hidden[pl.ds(s * reqs, reqs), :] = hidden_ref[s].astype(f32)
+    block = hidden[...]
+    factor = lax.rsqrt(jnp.mean(block * block, axis=-1, keepdims=True) + 1e-05)
+    normed[...] = (block * factor * gain_ref[...].astype(f32)).astype(bf16)
+
+    own_lengths = [lengths_ref[inst * reqs + r] for r in range(reqs)]
+
+    def by_request(index, numbers):
+        chosen = jnp.full(index.shape, numbers[0], jnp.int32)
+        for r in range(1, reqs):
+            chosen = jnp.where(index == r, numbers[r], chosen)
+        return chosen
+
+    row = lax.broadcasted_iota(jnp.int32, (rows, HEAD_SIZE), 0)
+    lane = lax.broadcasted_iota(jnp.int32, (rows, HEAD_SIZE), 1)
+    half = HEAD_SIZE // 2
+    place = (by_request(row & (reqs - 1), own_lengths) + row // reqs).astype(f32)
+    freqs = jnp.exp((lane & (half - 1)).astype(f32) * (-2.0 * math.log(THETA) / HEAD_SIZE))
+    angle = place * freqs
+    cosine = jnp.cos(angle)
+    sine = jnp.where(lane < half, -1.0, 1.0) * jnp.sin(angle)
+
+    def rotated(tensor):
+        return (tensor * cosine + pltpu.roll(tensor, half, 1) * sine).astype(bf16)
+
+    cache_copy.wait()
+    for j in range(2):
+        moved_out[j] = cache[leaving_ref[inst, j]]
+    pl.semaphore_wait(barrier, n)
+
+    def pair(src, dst, k):
+        return pltpu.make_async_remote_copy(
+            src_ref=src,
+            dst_ref=dst,
+            send_sem=pair_send.at[k],
+            recv_sem=pair_recv.at[k],
+            device_id={"inst": other},
+            device_id_type=MESH,
+        )
+
+    moving = pair(moved_out, moved_in, 0)
+    moving.start()
+
+    def query_copy(c, owner, p):
+        return pltpu.make_async_remote_copy(
+            src_ref=query_all.at[c, owner],
+            dst_ref=query_all.at[c, owner],
+            send_sem=query_send.at[c, p],
+            recv_sem=query_recv.at[c, owner],
+            device_id={"tp": p},
+            device_id_type=MESH,
+        )
+
+    for c in range(chunks):
+        total = jnp.zeros((rows, chunk_cols), f32)
+        for k in range(pieces):
+            wq_copies[c, k].wait()
+            total += jnp.dot(
+                normed[:, k * piece : (k + 1) * piece],
+                wq[k * piece : (k + 1) * piece, c * chunk_cols : (c + 1) * chunk_cols],
+                preferred_element_type=f32,
+            )
+        total = total.astype(bf16).astype(f32)
+        for h in range(chunk_heads):
+            query_all[c, me, h * rows : (h + 1) * rows, :] = rotated(
+                total[:, h * HEAD_SIZE : (h + 1) * HEAD_SIZE]
+            )
+        each_peer(lambda p: query_copy(c, me, p).start())
+
+    moving.wait_recv()
+    first, second = leaving_ref[inst, 0], leaving_ref[inst, 1]
+    for r in range(reqs):
+        leaves = jnp.logical_or(first == r, second == r)
+        fresh = moved_in[jnp.where(second == r, 1, 0)]
+        now = jnp.where(leaves, fresh, cache[r])
+        for k in range(n):
+            keys[k, r * positions : (r + 1) * positions, :] = now[
+                :, k * HEAD_SIZE : (k + 1) * HEAD_SIZE
+            ]
+            values[k, r * positions : (r + 1) * positions, :] = now[
+                :, kv_width + k * HEAD_SIZE : kv_width + (k + 1) * HEAD_SIZE
+            ]
+
+    wk_copy.wait()
+    key_new = jnp.dot(normed[...], wk[...], preferred_element_type=f32).astype(bf16)
+    key_new = rotated(key_new.astype(f32))
+    wv_copy.wait()
+    value_new = jnp.dot(normed[...], wv[...], preferred_element_type=f32).astype(bf16)
+
+    def page_of(index):
+        page = table_ref[adapter_ref[index]]
+        return jnp.clip(page - inst * store, 0, store - 1), page // store == inst
+
+    down_copy.wait()
+    up_copy.wait()
+    for r in range(reqs):
+        local, _ = page_of(other * reqs + r)
+        down_out[r] = down[local]
+        up_out[r] = up[local]
+    down_pair = pair(down_out, down_in, 1)
+    up_pair = pair(up_out, up_in, 2)
+    down_pair.start()
+    up_pair.start()
+
+    chunk_rows = chunk_heads * rows
+    wide = (chunk_rows, reqs * positions)
+    row = lax.broadcasted_iota(jnp.int32, wide, 0)
+    column = lax.broadcasted_iota(jnp.int32, wide, 1)
+    request = column // positions
+    at = me * positions + (column & (positions - 1))
+    valid = (request == (row & (reqs - 1))) & (at < by_request(request, own_lengths))
+    stat_lane = lax.broadcasted_iota(jnp.int32, (chunk_rows, 128), 1)
+
+    def attend(query, key, value, mask):
+        score = lax.dot_general(
+            query, key, (((1,), (1,)), ((), ())), preferred_element_type=f32
+        )
+        score = jnp.where(mask, score * inverse, NEGATIVE)
+        top = jnp.max(score, axis=-1, keepdims=True)
+        weight = jnp.where(mask, jnp.exp(score - top), 0.0)
+        total = jnp.sum(weight, axis=-1, keepdims=True)
+        mixed = jnp.dot(weight.astype(bf16), value, preferred_element_type=f32)
+        total = jnp.where(total > 0.0, total, 1.0)
+        return mixed / total, top + jnp.log(total)
+
+    def part_copy(c, owner, p):
+        return pltpu.make_async_remote_copy(
+            src_ref=part_out.at[c, p],
+            dst_ref=part_in.at[c, owner],
+            send_sem=part_send.at[c, p],
+            recv_sem=part_recv.at[c, owner],
+            device_id={"tp": p},
+            device_id_type=MESH,
+        )
+
+    stat[...] = jnp.zeros_like(stat)
+    for c in range(chunks):
+
+        def one_head(p):
+            mixed, level = attend(query_all[c, p], keys[p], values[p], valid)
+            at = pl.ds(c * chunk_rows, chunk_rows)
+            stat[at, :] = jnp.where(stat_lane == p, level, stat[at, :])
+            return mixed.astype(bf16)
+
+        def peer_head(p):
+            query_copy(c, p, p).wait_recv()
+            part_out[c, p] = one_head(p)
+            part_copy(c, me, p).start()
+
+        each_peer(peer_head)
+        part_in[c, me] = one_head(me)
+
+    def stat_copy(owner, p):
+        return pltpu.make_async_remote_copy(
+            src_ref=stat_out.at[p],
+            dst_ref=stat_in.at[owner],
+            send_sem=stat_send.at[p],
+            recv_sem=stat_recv.at[owner],
+            device_id={"tp": p},
+            device_id_type=MESH,
+        )
+
+    turned = jnp.transpose(stat[...])
+    for p in range(n):
+        stat_out[p] = jnp.broadcast_to(turned[p : p + 1, :], (8, 128))
+    stat_in[me] = stat_out[me]
+    each_peer(lambda p: stat_copy(me, p).start())
+
+    small = (chunk_rows, rows)
+    row = lax.broadcasted_iota(jnp.int32, small, 0)
+    column = lax.broadcasted_iota(jnp.int32, small, 1)
+    causal = ((row & (reqs - 1)) == (column & (reqs - 1))) & (
+        column // reqs <= (row & (rows - 1)) // reqs
+    )
+    fresh_parts = [attend(query_all[c, me], key_new, value_new, causal) for c in range(chunks)]
+
+    down_pair.wait_recv()
+    up_pair.wait_recv()
+    for r in range(reqs):
+        local, held = page_of(inst * reqs + r)
+        down_in[r] = jnp.where(held, down[local], down_in[r])
+        up_in[r] = jnp.where(held, up[local], up_in[r])
+
+    each_peer(lambda p: stat_copy(p, p).wait_recv())
+    sub = lax.broadcasted_iota(jnp.int32, (8, 128), 0)
+    levels = jnp.zeros((8, 128), f32)
+    for p in range(n):
+        levels = jnp.where(sub == p, stat_in[p], levels)
+    levels = jnp.transpose(levels)
+    for c in range(chunks):
+        each_peer(lambda p: part_copy(c, p, p).wait_recv())
+    heads = []
+    for c in range(chunks):
+        fresh_mixed, fresh_level = fresh_parts[c]
+        level = levels[c * chunk_rows : (c + 1) * chunk_rows, :]
+        top = jnp.maximum(jnp.max(level, axis=-1, keepdims=True), fresh_level)
+        weight = jnp.exp(level - top)
+        fresh_weight = jnp.exp(fresh_level - top)
+        total = jnp.sum(weight, axis=-1, keepdims=True) + fresh_weight
+        mixed = fresh_mixed * fresh_weight
+        for p in range(n):
+            mixed += part_in[c, p].astype(f32) * weight[:, p : p + 1]
+        mixed = (mixed / total).astype(bf16)
+        heads += [mixed[h * rows : (h + 1) * rows, :] for h in range(chunk_heads)]
+    attended = jnp.concatenate(heads, axis=1)
+
+    def shrink_copy(owner, p):
+        return pltpu.make_async_remote_copy(
+            src_ref=shrink_part,
+            dst_ref=shrink_in.at[owner],
+            send_sem=shrink_send.at[p],
+            recv_sem=shrink_recv.at[owner],
+            device_id={"tp": p},
+            device_id_type=MESH,
+        )
+
+    row = lax.broadcasted_iota(jnp.int32, (rows, rank), 0) & (reqs - 1)
+    shrunk = jnp.zeros((rows, rank), f32)
+    for r in range(reqs):
+        product = jnp.dot(attended, down_in[r], preferred_element_type=f32)
+        shrunk = jnp.where(row == r, product, shrunk)
+    shrink_part[...] = shrunk
+    each_peer(lambda p: shrink_copy(me, p).start())
+
+    def base_copy(owner, p):
+        return pltpu.make_async_remote_copy(
+            src_ref=base_out.at[p],
+            dst_ref=base_in.at[owner],
+            send_sem=base_send.at[p],
+            recv_sem=base_recv.at[owner],
+            device_id={"tp": p},
+            device_id_type=MESH,
+        )
+
+    def peer_block(p):
+        wo_copy(p).wait()
+        base_out[p] = jnp.dot(attended, wo[p], preferred_element_type=f32).astype(bf16)
+        base_copy(me, p).start()
+
+    each_peer(peer_block)
+    wo_copy(me).wait()
+    output = jnp.dot(attended, wo[me], preferred_element_type=f32)
+
+    each_peer(lambda p: shrink_copy(p, p).wait_recv())
+    shrink_in[me] = shrink_part[...]
+    shrunk = shrink_in[0]
+    for p in range(1, n):
+        shrunk += shrink_in[p]
+    shrunk = shrunk.astype(bf16)
+    delta = jnp.zeros((rows, out_cols), f32)
+    for r in range(reqs):
+        chosen = jnp.where(row == r, shrunk.astype(f32), 0.0).astype(bf16)
+        delta += jnp.dot(chosen, up_in[r], preferred_element_type=f32)
+    output += ADAPTER_SCALE * delta
+    hidden[:, :out_cols] = output
+
+    def add_block(p):
+        base_copy(p, p).wait_recv()
+        hidden[:, :out_cols] += base_in[p].astype(f32)
+
+    each_peer(add_block)
+    for s in range(steps):
+        out_ref[s] = hidden[pl.ds(s * reqs, reqs), :out_cols].astype(bf16)
+
+    moving.wait_send()
+    down_pair.wait_send()
+    up_pair.wait_send()
+
+    def sent(p):
+        for c in range(chunks):
+            query_copy(c, me, p).wait_send()
+            part_copy(c, me, p).wait_send()
+        stat_copy(me, p).wait_send()
+        shrink_copy(me, p).wait_send()
+        base_copy(me, p).wait_send()
+
+    each_peer(sent)
+
+
+CHUNKS = 2
+PIECES = 4
+
+
+def fused(
+    hidden_input,
+    input_norm_gain,
+    query_weight,
+    key_weight,
+    value_weight,
+    output_weight,
+    key_value_cache,
+    lengths,
+    leaving,
+    request_adapter_index,
+    adapter_page_table,
+    adapter_down_pages,
+    adapter_up_pages,
+):
+    n = lax.axis_size("tp")
+    steps, reqs, width = hidden_input.shape
+    head_cols = query_weight.shape[1]
+    positions, kv_both = key_value_cache.shape[1:]
+    store, _, rank = adapter_down_pages.shape
+    out_cols = adapter_up_pages.shape[2]
+    rows = steps * reqs
+    chunk_rows = head_cols // HEAD_SIZE // CHUNKS * rows
+    dims = (n, steps, reqs, width, head_cols, positions, store, rank, out_cols, CHUNKS, PIECES)
+    bf16, f32 = jnp.bfloat16, jnp.float32
+    dma = pltpu.SemaphoreType.DMA
+    vmem = pl.BlockSpec(memory_space=pltpu.VMEM)
+    smem = pl.BlockSpec(memory_space=pltpu.SMEM)
+    hbm = pl.BlockSpec(memory_space=pl.ANY)
+    return pl.pallas_call(
+        functools.partial(fused_kernel, dims),
+        out_shape=jax.ShapeDtypeStruct((steps, reqs, out_cols), bf16),
+        in_specs=[vmem, vmem, hbm, hbm, hbm, hbm, hbm, smem, smem, smem, smem, hbm, hbm],
+        out_specs=vmem,
+        scratch_shapes=[
+            pltpu.VMEM((width, head_cols), bf16),
+            pltpu.VMEM((width, HEAD_SIZE), bf16),
+            pltpu.VMEM((width, HEAD_SIZE), bf16),
+            pltpu.VMEM((n, head_cols, out_cols), bf16),
+            pltpu.VMEM((reqs, positions, kv_both), bf16),
+            pltpu.VMEM((2, positions, kv_both), bf16),
+            pltpu.VMEM((2, positions, kv_both), bf16),
+            pltpu.VMEM((n, reqs * positions, HEAD_SIZE), bf16),
+            pltpu.VMEM((n, reqs * positions, HEAD_SIZE), bf16),
+            pltpu.VMEM((store, head_cols, rank), bf16),
+            pltpu.VMEM((store, rank, out_cols), bf16),
+            pltpu.VMEM((reqs, head_cols, rank), bf16),
+            pltpu.VMEM((reqs, rank, out_cols), bf16),
+            pltpu.VMEM((reqs, head_cols, rank), bf16),
+            pltpu.VMEM((reqs, rank, out_cols), bf16),
+            pltpu.VMEM((rows, width), f32),
+            pltpu.VMEM((rows, width), bf16),
+            pltpu.VMEM((CHUNKS, n, chunk_rows, HEAD_SIZE), bf16),
+            pltpu.VMEM((CHUNKS, n, chunk_rows, HEAD_SIZE), bf16),
+            pltpu.VMEM((CHUNKS, n, chunk_rows, HEAD_SIZE), bf16),
+            pltpu.VMEM((CHUNKS * chunk_rows, 128), f32),
+            pltpu.VMEM((n, 8, 128), f32),
+            pltpu.VMEM((n, 8, 128), f32),
+            pltpu.VMEM((rows, rank), f32),
+            pltpu.VMEM((n, rows, rank), f32),
+            pltpu.VMEM((n, rows, out_cols), bf16),
+            pltpu.VMEM((n, rows, out_cols), bf16),
+            dma((CHUNKS, PIECES)),
+            dma((2,)),
+            dma((n,)),
+            dma((3,)),
+            dma((3,)),
+            dma((3,)),
+            dma((CHUNKS, n)),
+            dma((CHUNKS, n)),
+            dma((CHUNKS, n)),
+            dma((CHUNKS, n)),
+            dma((n,)),
+            dma((n,)),
+            dma((n,)),
+            dma((n,)),
+            dma((n,)),
+            dma((n,)),
+        ],
+        compiler_params=pltpu.CompilerParams(
+            collective_id=0, has_side_effects=True, vmem_limit_bytes=60 * 1024 * 1024
+        ),
+        name="fused",
+    )(
+        hidden_input,
+        input_norm_gain.reshape(1, width),
+        query_weight,
+        key_weight,
+        value_weight,
+        output_weight,
+        key_value_cache,
+        lengths,
+        leaving,
+        request_adapter_index,
+        adapter_page_table,
+        adapter_down_pages,
+        adapter_up_pages,
+    )
+
+
 def solution(mesh):
+    body = fused if mesh.shape["tp"] == KVH and mesh.shape["inst"] == 2 else shards
     return jax.shard_map(
-        shards,
+        body,
         mesh=mesh,
         in_specs=(
             P(None, ("groups", "inst"), None),

time: 295 us -> 42.1 us (0.14)
  blocking collectives: 165 us -> 0 us
  waiting for transfers between devices: 37 us -> 0 us
  Pallas kernels: 0 us -> 34.3 us
  local copies, waits for them, and re-layouts: 32.2 us -> 7.52 us
  matrix products: 24.3 us -> 0 us
  other arithmetic: 21.3 us -> 0 us
  between operations: 13.8 us -> 0.01 us
    all_gather x5 -> x0, blocking collectives: 146 us -> none  [the longest x2 61.1 us: combined_all(): lax.all_gather(part.astype(kind), axis)]
    reduce_scatter x1 -> x0, waiting for transfers between devices: 36.9 us -> none  [shards(): lax.psum_scatter(base_part.astype(jnp.bfloat16), 'tp', scatter_dimension=...]
    pallas_call x0 -> x1, Pallas kernels: none -> 34.3 us  [fused(): pl.pallas_call(functools.partial(fused_kernel, dims), out_shape=jax.Shape...]
    dot_general x10 -> x0, matrix products: 24.3 us -> none  [the longest x1 8.8 us: shards(): jnp.dot(attention_output, output_weight, preferred_element_type=jnp.float32)]
    psum x1 -> x0, blocking collectives: 18.9 us -> none  [shards(): shrunk_output = lax.psum(shrink_part, 'tp')]
    gather x8 -> x0, local copies, waits for them, and re-layouts: 13.7 us -> none  [the longest x2 6.03 us: select_pages(): adapter_up_pages[local_page_index].reshape(request_rows, -1)]
    add x15 -> x0, other arithmetic: 10.4 us -> none  [the longest x7 10.2 us: combine(): mixed_first * scale_first[..., None]]
    reshape x7 -> x1, local copies, waits for them, and re-layouts: 7.2 us -> 1.35 us  [fused(): input_norm_gain.reshape(1, width)]
  transfers between devices with their start and end apart: 4 -> 0, of which waited for: 1 -> 0; matrix products, arithmetic and copies ran while one was open for 17% -> 0% of each run, Pallas kernels for 0% -> 0%
where the time goes in v1:
time: 42.1 us; the launch traced here: 41.8 us
  Pallas kernels  34.3 us (81%)
  local copies, waits for them, and re-layouts  7.52 us (18%)
    pallas_call x1, Pallas kernels, fused(): pl.pallas_call(functools.partial(fused_kernel, dims), out_shape=jax.Shape...  34.3 us
    unnamed x2, local copies, waits for them, and re-layouts  6.17 us
    reshape x1, local copies, waits for them, and re-layouts, fused(): input_norm_gain.reshape(1, width)  1.35 us

profile of v1, /device:TPU:0, one launch (start us, length us, event | category | flops | bytes accessed | tf_op | source)
XLA Modules:
  0.0 41.8 jit_solution(4890342075469231295)
XLA Ops:
  0.0 1.3 %reshape.3.gain_ref = bf16[1,8192]{1,0:T(2,128)(2,1)} reshape(bf16[8192]{0:T(1024)(128)(2,1)} %param.14) | data formatting | bytes 32768 | tf_op jit(solution)/shard_map/reshape | solution.py:708
  1.4 4.8 %copy.14.down_hbm = bf16[16,1024,64]{2,1,0:T(8,128)(2,1)} copy(bf16[16,1024,64]{1,2,0:T(8,128)(2,1)} %param.24) | data formatting | bytes 4194304 | tf_op args[11]
  6.1 34.3 %fused.1 = bf16[4,4,1024]{2,1,0:T(4,128)(2,1)} custom-call(bf16[4,4,8192]{2,1,0:T(4,128)(2,1)} %hidden_ref.1, bf16[1,8192]{1,0:T(2,128)(2,1)} %reshape.3.gain_ref, bf16[8192,1024]{1,0:T(8,128)(2,1)} %wq_hbm.1, bf16[8192,128]{1,0:T(8,128)(2,1)} %wk_hbm.1, bf16[8192,128]{1,0:T(8,128)(2,1)} %wv_hbm.1, bf16[1024,8192]{1,0:T(8,128)(2,1)} %wo_hbm.1, ...), custom_call_target="tpu_custom_call" | custom-call | tf_op jit(solution)/shard_map/fused/pallas_call | solution.py:652
  40.4 1.4 %copy.16 = bf16[4,4,1024]{2,1,0:T(4,128)(2,1)} copy(bf16[4,4,1024]{2,1,0:T(4,128)(2,1)} %fused.1) | data formatting | bytes 65536

commit v2 on v1

--- a/solution.py
+++ b/solution.py
@@ -340,7 +340,10 @@
         hidden[pl.ds(s * reqs, reqs), :] = hidden_ref[s].astype(f32)
     block = hidden[...]
     factor = lax.rsqrt(jnp.mean(block * block, axis=-1, keepdims=True) + 1e-05)
-    normed[...] = (block * factor * gain_ref[...].astype(f32)).astype(bf16)
+    gain = gain_ref[...].astype(f32)
+    for i in range(width // 128):
+        cols = slice(i * 128, (i + 1) * 128)
+        normed[:, cols] = (hidden[:, cols] * factor * gain[i : i + 1, :]).astype(bf16)
 
     own_lengths = [lengths_ref[inst * reqs + r] for r in range(reqs)]
 
@@ -365,7 +368,6 @@
     cache_copy.wait()
     for j in range(2):
         moved_out[j] = cache[leaving_ref[inst, j]]
-    pl.semaphore_wait(barrier, n)
 
     def pair(src, dst, k):
         return pltpu.make_async_remote_copy(
@@ -378,7 +380,6 @@
         )
 
     moving = pair(moved_out, moved_in, 0)
-    moving.start()
 
     def query_copy(c, owner, p):
         return pltpu.make_async_remote_copy(
@@ -404,6 +405,9 @@
             query_all[c, me, h * rows : (h + 1) * rows, :] = rotated(
                 total[:, h * HEAD_SIZE : (h + 1) * HEAD_SIZE]
             )
+        if c == 0:
+            pl.semaphore_wait(barrier, n)
+            moving.start()
         each_peer(lambda p: query_copy(c, me, p).start())
 
     moving.wait_recv()
@@ -472,22 +476,22 @@
             device_id_type=MESH,
         )
 
-    stat[...] = jnp.zeros_like(stat)
     for c in range(chunks):
-
-        def one_head(p):
-            mixed, level = attend(query_all[c, p], keys[p], values[p], valid)
-            at = pl.ds(c * chunk_rows, chunk_rows)
-            stat[at, :] = jnp.where(stat_lane == p, level, stat[at, :])
-            return mixed.astype(bf16)
-
-        def peer_head(p):
-            query_copy(c, p, p).wait_recv()
-            part_out[c, p] = one_head(p)
-            part_copy(c, me, p).start()
-
-        each_peer(peer_head)
-        part_in[c, me] = one_head(me)
+        levels = jnp.zeros((chunk_rows, 128), f32)
+        for begin in range(0, n, 4):
+            some = [lax.rem(me + o, n) for o in range(begin, begin + 4)]
+            for p in some:
+                if p is not some[0] or begin > 0:
+                    query_copy(c, p, p).wait_recv()
+            mixed = [attend(query_all[c, p], keys[p], values[p], valid) for p in some]
+            for p, (part, level) in zip(some, mixed):
+                levels = jnp.where(stat_lane == p, level, levels)
+                if p is not some[0] or begin > 0:
+                    part_out[c, p] = part.astype(bf16)
+                    part_copy(c, me, p).start()
+                else:
+                    part_in[c, me] = part.astype(bf16)
+        stat[c * chunk_rows : (c + 1) * chunk_rows, :] = levels
 
     def stat_copy(owner, p):
         return pltpu.make_async_remote_copy(
@@ -556,7 +560,9 @@
     row = lax.broadcasted_iota(jnp.int32, (rows, rank), 0) & (reqs - 1)
     shrunk = jnp.zeros((rows, rank), f32)
     for r in range(reqs):
-        product = jnp.dot(attended, down_in[r], preferred_element_type=f32)
+        product = lax.dot_general(
+            attended, down_in[r], (((1,), (1,)), ((), ())), preferred_element_type=f32
+        )
         shrunk = jnp.where(row == r, product, shrunk)
     shrink_part[...] = shrunk
     each_peer(lambda p: shrink_copy(me, p).start())
@@ -591,13 +597,11 @@
         chosen = jnp.where(row == r, shrunk.astype(f32), 0.0).astype(bf16)
         delta += jnp.dot(chosen, up_in[r], preferred_element_type=f32)
     output += ADAPTER_SCALE * delta
+    each_peer(lambda p: base_copy(p, p).wait_recv())
+    base_in[me] = jnp.zeros((rows, out_cols), bf16)
+    for p in range(n):
+        output += base_in[p].astype(f32)
     hidden[:, :out_cols] = output
-
-    def add_block(p):
-        base_copy(p, p).wait_recv()
-        hidden[:, :out_cols] += base_in[p].astype(f32)
-
-    each_peer(add_block)
     for s in range(steps):
         out_ref[s] = hidden[pl.ds(s * reqs, reqs), :out_cols].astype(bf16)
 
@@ -664,11 +668,11 @@
             pltpu.VMEM((2, positions, kv_both), bf16),
             pltpu.VMEM((n, reqs * positions, HEAD_SIZE), bf16),
             pltpu.VMEM((n, reqs * positions, HEAD_SIZE), bf16),
-            pltpu.VMEM((store, head_cols, rank), bf16),
+            pltpu.VMEM((store, rank, head_cols), bf16),
             pltpu.VMEM((store, rank, out_cols), bf16),
-            pltpu.VMEM((reqs, head_cols, rank), bf16),
+            pltpu.VMEM((reqs, rank, head_cols), bf16),
             pltpu.VMEM((reqs, rank, out_cols), bf16),
-            pltpu.VMEM((reqs, head_cols, rank), bf16),
+            pltpu.VMEM((reqs, rank, head_cols), bf16),
             pltpu.VMEM((reqs, rank, out_cols), bf16),
             pltpu.VMEM((rows, width), f32),
             pltpu.VMEM((rows, width), bf16),
@@ -705,7 +709,7 @@
         name="fused",
     )(
         hidden_input,
-        input_norm_gain.reshape(1, width),
+        input_norm_gain.reshape(width // 128, 128),
         query_weight,
         key_weight,
         value_weight,
@@ -715,7 +719,7 @@
         leaving,
         request_adapter_index,
         adapter_page_table,
-        adapter_down_pages,
+        jnp.swapaxes(adapter_down_pages, 1, 2),
         adapter_up_pages,
     )
 

time: 42.1 us -> 36.4 us (0.86)
  local copies, waits for them, and re-layouts: 7.52 us -> 1.39 us
  Pallas kernels: 34.3 us -> 34.8 us
    unnamed x2 -> x1, local copies, waits for them, and re-layouts: 6.17 us -> 1.39 us
    reshape x1 -> x0, local copies, waits for them, and re-layouts: 1.35 us -> none  [fused(): input_norm_gain.reshape(1, width)]
    pallas_call x1, Pallas kernels: 34.3 us -> 34.8 us  [fused(): pl.pallas_call(functools.partial(fused_kernel, dims), out_shape=jax.Shape...]
where the time goes in v2:
time: 36.4 us; the launch traced here: 36.2 us
  Pallas kernels  34.8 us (96%)
  local copies, waits for them, and re-layouts  1.39 us (4%)
    pallas_call x1, Pallas kernels, fused(): pl.pallas_call(functools.partial(fused_kernel, dims), out_shape=jax.Shape...  34.8 us
    unnamed x1, local copies, waits for them, and re-layouts  1.39 us

profile of v2, /device:TPU:0, one launch (start us, length us, event | category | flops | bytes accessed | tf_op | source)
XLA Modules:
  0.0 36.2 jit_solution(21763856975519308)
XLA Ops:
  0.0 34.8 %fused.1 = bf16[4,4,1024]{2,1,0:T(4,128)(2,1)} custom-call(bf16[4,4,8192]{2,1,0:T(4,128)(2,1)} %hidden_ref.1, bf16[64,128]{1,0:T(8,128)(2,1)} %bitcast.3, bf16[8192,1024]{1,0:T(8,128)(2,1)} %wq_hbm.1, bf16[8192,128]{1,0:T(8,128)(2,1)} %wk_hbm.1, bf16[8192,128]{1,0:T(8,128)(2,1)} %wv_hbm.1, bf16[1024,8192]{1,0:T(8,128)(2,1)} %wo_hbm.1, ...), custom_call_target="tpu_custom_call" | custom-call | tf_op jit(solution)/shard_map/fused/pallas_call | solution.py:656
  34.8 1.4 %copy.15 = bf16[4,4,1024]{2,1,0:T(4,128)(2,1)} copy(bf16[4,4,1024]{2,1,0:T(4,128)(2,1)} %fused.1) | data formatting | bytes 65536

commit v3 on v2

--- a/solution.py
+++ b/solution.py
@@ -259,9 +259,6 @@
     query_all,
     part_out,
     part_in,
-    stat,
-    stat_out,
-    stat_in,
     shrink_part,
     shrink_in,
     base_out,
@@ -276,8 +273,6 @@
     query_recv,
     part_send,
     part_recv,
-    stat_send,
-    stat_recv,
     shrink_send,
     shrink_recv,
     base_send,
@@ -296,15 +291,13 @@
     f32, bf16 = jnp.float32, jnp.bfloat16
     inverse = 1.0 / math.sqrt(HEAD_SIZE)
 
+    order = [lax.rem(me + o, n) for o in range(n)]
+
     def each_peer(body):
-        def step(o, carry):
-            body(lax.rem(me + 1 + o, n))
-            return carry
-
-        lax.fori_loop(0, n - 1, step, 0)
+        for p in order[1:]:
+            body(p)
 
     cache_copy = pltpu.make_async_copy(cache_hbm, cache, store_sem.at[0])
-    cache_copy.start()
     wq_copies = {}
     for c in range(chunks):
         for k in range(pieces):
@@ -313,6 +306,8 @@
                 wq_hbm.at[at], wq.at[at], wq_sem.at[c, k]
             )
             wq_copies[c, k].start()
+        if c == 0:
+            cache_copy.start()
     wk_copy = pltpu.make_async_copy(wk_hbm, wk, wkv_sem.at[0])
     wv_copy = pltpu.make_async_copy(wv_hbm, wv, wkv_sem.at[1])
     down_copy = pltpu.make_async_copy(down_hbm, down, store_sem.at[1])
@@ -365,9 +360,6 @@
     def rotated(tensor):
         return (tensor * cosine + pltpu.roll(tensor, half, 1) * sine).astype(bf16)
 
-    cache_copy.wait()
-    for j in range(2):
-        moved_out[j] = cache[leaving_ref[inst, j]]
 
     def pair(src, dst, k):
         return pltpu.make_async_remote_copy(
@@ -407,8 +399,12 @@
             )
         if c == 0:
             pl.semaphore_wait(barrier, n)
+        each_peer(lambda p: query_copy(c, me, p).start())
+        if c == 0:
+            cache_copy.wait()
+            for j in range(2):
+                moved_out[j] = cache[leaving_ref[inst, j]]
             moving.start()
-        each_peer(lambda p: query_copy(c, me, p).start())
 
     moving.wait_recv()
     first, second = leaving_ref[inst, 0], leaving_ref[inst, 1]
@@ -424,11 +420,67 @@
                 :, kv_width + k * HEAD_SIZE : kv_width + (k + 1) * HEAD_SIZE
             ]
 
-    wk_copy.wait()
-    key_new = jnp.dot(normed[...], wk[...], preferred_element_type=f32).astype(bf16)
-    key_new = rotated(key_new.astype(f32))
-    wv_copy.wait()
-    value_new = jnp.dot(normed[...], wv[...], preferred_element_type=f32).astype(bf16)
+    chunk_rows = chunk_heads * rows
+    wide = (chunk_rows, reqs * positions)
+    row = lax.broadcasted_iota(jnp.int32, wide, 0)
+    column = lax.broadcasted_iota(jnp.int32, wide, 1)
+    request = column // positions
+    at = me * positions + (column & (positions - 1))
+    valid = (request == (row & (reqs - 1))) & (at < by_request(request, own_lengths))
+    stat_lane = lax.broadcasted_iota(jnp.int32, (chunk_rows, 128), 1)
+
+    def attend(query, key, value, mask):
+        score = lax.dot_general(
+            query, key, (((1,), (1,)), ((), ())), preferred_element_type=f32
+        )
+        score = jnp.where(mask, score * inverse, NEGATIVE)
+        top = jnp.max(score, axis=-1, keepdims=True)
+        weight = jnp.where(mask, jnp.exp(score - top), 0.0)
+        total = jnp.sum(weight, axis=-1, keepdims=True)
+        mixed = jnp.dot(weight.astype(bf16), value, preferred_element_type=f32)
+        total = jnp.where(total > 0.0, total, 1.0)
+        return mixed / total, top + jnp.log(total)
+
+    def part_copy(c, owner, p):
+        return pltpu.make_async_remote_copy(
+            src_ref=part_out.at[c, p],
+            dst_ref=part_in.at[c, owner],
+            send_sem=part_send.at[c, p],
+            recv_sem=part_recv.at[c, owner],
+            device_id={"tp": p},
+            device_id_type=MESH,
+        )
+
+    extra = lax.broadcasted_iota(jnp.int32, (16, 128), 0)
+
+    def attend_some(c, some):
+        for o in some:
+            if o > 0:
+                query_copy(c, order[o], order[o]).wait_recv()
+        parts = [attend(query_all[c, order[o]], keys[order[o]], values[order[o]], valid) for o in some]
+        levels = jnp.zeros((chunk_rows, 128), f32)
+        for o, (_, level) in zip(some, parts):
+            levels = jnp.where(stat_lane == o, level, levels)
+        if chunk_rows < 128:
+            levels = jnp.concatenate([levels, jnp.zeros((128 - chunk_rows, 128), f32)], axis=0)
+        levels = jnp.transpose(levels)
+        for o, (mixed, _) in zip(some, parts):
+            level = levels[o : o + 1, :]
+            high = level.astype(bf16).astype(f32)
+            middle = (level - high).astype(bf16).astype(f32)
+            low = level - high - middle
+            split = jnp.where(extra == 0, high, jnp.where(extra == 1, middle, jnp.where(extra == 2, low, 0.0)))
+            target = part_in.at[c, me] if o == 0 else part_out.at[c, order[o]]
+            target[:chunk_rows, :] = mixed.astype(bf16)
+            target[chunk_rows:, :] = split.astype(bf16)
+            if o > 0:
+                part_copy(c, me, order[o]).start()
+
+    def attend_chunk(c):
+        for begin in range(0, n, GROUP):
+            attend_some(c, range(begin, begin + GROUP))
+
+    attend_chunk(0)
 
     def page_of(index):
         page = table_ref[adapter_ref[index]]
@@ -445,69 +497,14 @@
     down_pair.start()
     up_pair.start()
 
-    chunk_rows = chunk_heads * rows
-    wide = (chunk_rows, reqs * positions)
-    row = lax.broadcasted_iota(jnp.int32, wide, 0)
-    column = lax.broadcasted_iota(jnp.int32, wide, 1)
-    request = column // positions
-    at = me * positions + (column & (positions - 1))
-    valid = (request == (row & (reqs - 1))) & (at < by_request(request, own_lengths))
-    stat_lane = lax.broadcasted_iota(jnp.int32, (chunk_rows, 128), 1)
-
-    def attend(query, key, value, mask):
-        score = lax.dot_general(
-            query, key, (((1,), (1,)), ((), ())), preferred_element_type=f32
-        )
-        score = jnp.where(mask, score * inverse, NEGATIVE)
-        top = jnp.max(score, axis=-1, keepdims=True)
-        weight = jnp.where(mask, jnp.exp(score - top), 0.0)
-        total = jnp.sum(weight, axis=-1, keepdims=True)
-        mixed = jnp.dot(weight.astype(bf16), value, preferred_element_type=f32)
-        total = jnp.where(total > 0.0, total, 1.0)
-        return mixed / total, top + jnp.log(total)
-
-    def part_copy(c, owner, p):
-        return pltpu.make_async_remote_copy(
-            src_ref=part_out.at[c, p],
-            dst_ref=part_in.at[c, owner],
-            send_sem=part_send.at[c, p],
-            recv_sem=part_recv.at[c, owner],
-            device_id={"tp": p},
-            device_id_type=MESH,
-        )
-
-    for c in range(chunks):
-        levels = jnp.zeros((chunk_rows, 128), f32)
-        for begin in range(0, n, 4):
-            some = [lax.rem(me + o, n) for o in range(begin, begin + 4)]
-            for p in some:
-                if p is not some[0] or begin > 0:
-                    query_copy(c, p, p).wait_recv()
-            mixed = [attend(query_all[c, p], keys[p], values[p], valid) for p in some]
-            for p, (part, level) in zip(some, mixed):
-                levels = jnp.where(stat_lane == p, level, levels)
-                if p is not some[0] or begin > 0:
-                    part_out[c, p] = part.astype(bf16)
-                    part_copy(c, me, p).start()
-                else:
-                    part_in[c, me] = part.astype(bf16)
-        stat[c * chunk_rows : (c + 1) * chunk_rows, :] = levels
-
-    def stat_copy(owner, p):
-        return pltpu.make_async_remote_copy(
-            src_ref=stat_out.at[p],
-            dst_ref=stat_in.at[owner],
-            send_sem=stat_send.at[p],
-            recv_sem=stat_recv.at[owner],
-            device_id={"tp": p},
-            device_id_type=MESH,
-        )
-
-    turned = jnp.transpose(stat[...])
-    for p in range(n):
-        stat_out[p] = jnp.broadcast_to(turned[p : p + 1, :], (8, 128))
-    stat_in[me] = stat_out[me]
-    each_peer(lambda p: stat_copy(me, p).start())
+    for c in range(1, chunks):
+        attend_chunk(c)
+
+    wk_copy.wait()
+    key_new = jnp.dot(normed[...], wk[...], preferred_element_type=f32).astype(bf16)
+    key_new = rotated(key_new.astype(f32))
+    wv_copy.wait()
+    value_new = jnp.dot(normed[...], wv[...], preferred_element_type=f32).astype(bf16)
 
     small = (chunk_rows, rows)
     row = lax.broadcasted_iota(jnp.int32, small, 0)
@@ -524,25 +521,24 @@
         down_in[r] = jnp.where(held, down[local], down_in[r])
         up_in[r] = jnp.where(held, up[local], up_in[r])
 
-    each_peer(lambda p: stat_copy(p, p).wait_recv())
-    sub = lax.broadcasted_iota(jnp.int32, (8, 128), 0)
-    levels = jnp.zeros((8, 128), f32)
-    for p in range(n):
-        levels = jnp.where(sub == p, stat_in[p], levels)
-    levels = jnp.transpose(levels)
     for c in range(chunks):
         each_peer(lambda p: part_copy(c, p, p).wait_recv())
+    sub = lax.broadcasted_iota(jnp.int32, (8, 128), 0)
     heads = []
     for c in range(chunks):
         fresh_mixed, fresh_level = fresh_parts[c]
-        level = levels[c * chunk_rows : (c + 1) * chunk_rows, :]
+        level = jnp.zeros((8, 128), f32)
+        for p in range(n):
+            split = jnp.sum(part_in[c, p, chunk_rows:, :].astype(f32), axis=0, keepdims=True)
+            level = jnp.where(sub == p, split, level)
+        level = jnp.transpose(level)[:chunk_rows, :]
         top = jnp.maximum(jnp.max(level, axis=-1, keepdims=True), fresh_level)
         weight = jnp.exp(level - top)
         fresh_weight = jnp.exp(fresh_level - top)
         total = jnp.sum(weight, axis=-1, keepdims=True) + fresh_weight
         mixed = fresh_mixed * fresh_weight
         for p in range(n):
-            mixed += part_in[c, p].astype(f32) * weight[:, p : p + 1]
+            mixed += part_in[c, p, :chunk_rows, :].astype(f32) * weight[:, p : p + 1]
         mixed = (mixed / total).astype(bf16)
         heads += [mixed[h * rows : (h + 1) * rows, :] for h in range(chunk_heads)]
     attended = jnp.concatenate(heads, axis=1)
@@ -597,6 +593,18 @@
         chosen = jnp.where(row == r, shrunk.astype(f32), 0.0).astype(bf16)
         delta += jnp.dot(chosen, up_in[r], preferred_element_type=f32)
     output += ADAPTER_SCALE * delta
+    moving.wait_send()
+    down_pair.wait_send()
+    up_pair.wait_send()
+
+    def sent(p):
+        for c in range(chunks):
+            query_copy(c, me, p).wait_send()
+            part_copy(c, me, p).wait_send()
+        shrink_copy(me, p).wait_send()
+
+    each_peer(sent)
+
     each_peer(lambda p: base_copy(p, p).wait_recv())
     base_in[me] = jnp.zeros((rows, out_cols), bf16)
     for p in range(n):
@@ -605,22 +613,11 @@
     for s in range(steps):
         out_ref[s] = hidden[pl.ds(s * reqs, reqs), :out_cols].astype(bf16)
 
-    moving.wait_send()
-    down_pair.wait_send()
-    up_pair.wait_send()
-
-    def sent(p):
-        for c in range(chunks):
-            query_copy(c, me, p).wait_send()
-            part_copy(c, me, p).wait_send()
-        stat_copy(me, p).wait_send()
-        shrink_copy(me, p).wait_send()
-        base_copy(me, p).wait_send()
-
-    each_peer(sent)
+    each_peer(lambda p: base_copy(me, p).wait_send())
 
 
 CHUNKS = 2
+GROUP = 8
 PIECES = 4
 
 
@@ -677,11 +674,8 @@
             pltpu.VMEM((rows, width), f32),
             pltpu.VMEM((rows, width), bf16),
             pltpu.VMEM((CHUNKS, n, chunk_rows, HEAD_SIZE), bf16),
-            pltpu.VMEM((CHUNKS, n, chunk_rows, HEAD_SIZE), bf16),
-            pltpu.VMEM((CHUNKS, n, chunk_rows, HEAD_SIZE), bf16),
-            pltpu.VMEM((CHUNKS * chunk_rows, 128), f32),
-            pltpu.VMEM((n, 8, 128), f32),
-            pltpu.VMEM((n, 8, 128), f32),
+            pltpu.VMEM((CHUNKS, n, chunk_rows + 16, HEAD_SIZE), bf16),
+            pltpu.VMEM((CHUNKS, n, chunk_rows + 16, HEAD_SIZE), bf16),
             pltpu.VMEM((rows, rank), f32),
             pltpu.VMEM((n, rows, rank), f32),
             pltpu.VMEM((n, rows, out_cols), bf16),
@@ -696,8 +690,6 @@
             dma((CHUNKS, n)),
             dma((CHUNKS, n)),
             dma((CHUNKS, n)),
-            dma((n,)),
-            dma((n,)),
             dma((n,)),
             dma((n,)),
             dma((n,)),

time: 36.4 us -> 34.6 us (0.951)
  Pallas kernels: 34.8 us -> 33 us
    pallas_call x1, Pallas kernels: 34.8 us -> 33 us  [fused(): pl.pallas_call(functools.partial(fused_kernel, dims), out_shape=jax.Shape...]
where the time goes in v3:
time: 34.6 us; the launch traced here: 34.4 us
  Pallas kernels  33 us (95%)
  local copies, waits for them, and re-layouts  1.39 us (4%)
    pallas_call x1, Pallas kernels, fused(): pl.pallas_call(functools.partial(fused_kernel, dims), out_shape=jax.Shape...  33 us
    unnamed x1, local copies, waits for them, and re-layouts  1.39 us

profile of v3, /device:TPU:0, one launch (start us, length us, event | category | flops | bytes accessed | tf_op | source)
XLA Modules:
  0.0 34.4 jit_solution(15573444345620611419)
XLA Ops:
  0.0 33.0 %fused.1 = bf16[4,4,1024]{2,1,0:T(4,128)(2,1)} custom-call(bf16[4,4,8192]{2,1,0:T(4,128)(2,1)} %hidden_ref.1, bf16[64,128]{1,0:T(8,128)(2,1)} %bitcast.3, bf16[8192,1024]{1,0:T(8,128)(2,1)} %wq_hbm.1, bf16[8192,128]{1,0:T(8,128)(2,1)} %wk_hbm.1, bf16[8192,128]{1,0:T(8,128)(2,1)} %wv_hbm.1, bf16[1024,8192]{1,0:T(8,128)(2,1)} %wo_hbm.1, ...), custom_call_target="tpu_custom_call" | custom-call | tf_op jit(solution)/shard_map/fused/pallas_call | solution.py:653
  33.0 1.4 %copy.15 = bf16[4,4,1024]{2,1,0:T(4,128)(2,1)} copy(bf16[4,4,1024]{2,1,0:T(4,128)(2,1)} %fused.1) | data formatting | bytes 65536

commit v4 on v3

--- a/solution.py
+++ b/solution.py
@@ -312,10 +312,6 @@
     wv_copy = pltpu.make_async_copy(wv_hbm, wv, wkv_sem.at[1])
     down_copy = pltpu.make_async_copy(down_hbm, down, store_sem.at[1])
     up_copy = pltpu.make_async_copy(up_hbm, up, store_sem.at[2])
-    wk_copy.start()
-    wv_copy.start()
-    down_copy.start()
-    up_copy.start()
 
     def wo_copy(p):
         cols = pl.ds(pl.multiple_of(p * out_cols, out_cols), out_cols)
@@ -325,7 +321,6 @@
         wo_copy(lax.rem(me + 1 + o, n)).start()
         return carry
 
-    lax.fori_loop(0, n, start_wo, 0)
 
     barrier = pltpu.get_barrier_semaphore()
     each_peer(lambda p: pl.semaphore_signal(barrier, inc=1, device_id={"tp": p}, device_id_type=MESH))
@@ -406,6 +401,10 @@
                 moved_out[j] = cache[leaving_ref[inst, j]]
             moving.start()
 
+    wk_copy.start()
+    wv_copy.start()
+    down_copy.start()
+    up_copy.start()
     moving.wait_recv()
     first, second = leaving_ref[inst, 0], leaving_ref[inst, 1]
     for r in range(reqs):
@@ -500,6 +499,7 @@
     for c in range(1, chunks):
         attend_chunk(c)
 
+    lax.fori_loop(0, n, start_wo, 0)
     wk_copy.wait()
     key_new = jnp.dot(normed[...], wk[...], preferred_element_type=f32).astype(bf16)
     key_new = rotated(key_new.astype(f32))

time: 34.6 us -> 34.1 us (0.986)
  Pallas kernels: 33 us -> 32.5 us
    pallas_call x1, Pallas kernels: 33 us -> 32.5 us  [fused(): pl.pallas_call(functools.partial(fused_kernel, dims), out_shape=jax.Shape...]
where the time goes in v4:
time: 34.1 us; the launch traced here: 33.9 us
  Pallas kernels  32.5 us (95%)
  local copies, waits for them, and re-layouts  1.39 us (4%)
    pallas_call x1, Pallas kernels, fused(): pl.pallas_call(functools.partial(fused_kernel, dims), out_shape=jax.Shape...  32.5 us
    unnamed x1, local copies, waits for them, and re-layouts  1.39 us

profile of v4, /device:TPU:0, one launch (start us, length us, event | category | flops | bytes accessed | tf_op | source)
XLA Modules:
  0.0 33.9 jit_solution(17098176699125718519)
XLA Ops:
  0.0 32.5 %fused.1 = bf16[4,4,1024]{2,1,0:T(4,128)(2,1)} custom-call(bf16[4,4,8192]{2,1,0:T(4,128)(2,1)} %hidden_ref.1, bf16[64,128]{1,0:T(8,128)(2,1)} %bitcast.3, bf16[8192,1024]{1,0:T(8,128)(2,1)} %wq_hbm.1, bf16[8192,128]{1,0:T(8,128)(2,1)} %wk_hbm.1, bf16[8192,128]{1,0:T(8,128)(2,1)} %wv_hbm.1, bf16[1024,8192]{1,0:T(8,128)(2,1)} %wo_hbm.1, ...), custom_call_target="tpu_custom_call" | custom-call | tf_op jit(solution)/shard_map/fused/pallas_call | solution.py:653
  32.5 1.4 %copy.15 = bf16[4,4,1024]{2,1,0:T(4,128)(2,1)} copy(bf16[4,4,1024]{2,1,0:T(4,128)(2,1)} %fused.1) | data formatting | bytes 65536
